TPU v7x, 256 devices: a whole 4x4x8 slice. The times are simulated.
256 devices in a mesh: row: 8 (over z), col: 32 (over y, x, core).
Axes of the slice: x: 4, y: 4, z: 8, core: 2. Of those that a mesh axis runs over, the one named last changes fastest.
Arguments:
- queries: bfloat16 [32, 1024, 6144], P('col', 'row'), may hold values from -6 to 6
- keys: bfloat16 [32, 1024, 6144], P('col', 'row'), may hold values from -6 to 6
- values: bfloat16 [32, 1024, 6144], P('col', 'row'), may hold values from -6 to 6
- query_gain: float32 [6144], replicated, may hold values from 1 to 2.2
- key_gain: float32 [6144], replicated, may hold values from 1 to 2.2
- cotangent: bfloat16 [32, 1024, 6144], P('col', 'row'), may hold values from -18 to 18
Outputs:
- attended: bfloat16 [32, 1024, 6144], P('col', 'row')
- query_grad: bfloat16 [32, 1024, 6144], P('col', 'row')
- key_grad: bfloat16 [32, 1024, 6144], P('col', 'row')
- value_grad: bfloat16 [32, 1024, 6144], P('col', 'row')
- query_gain_grad: float32 [6144], replicated
- key_gain_grad: float32 [6144], replicated
All inputs are finite; a program needn't handle non-finite values.
Results may differ from a plain program's by a relative error of at most 0.012.
The roundings to bfloat16 on the way count: a program that leaves them out, or rounds other values in their place, can miss the bound.
Values may be sent and summed in bfloat16 or wider, within the bound.
A program may use at most 128 MiB of HBM per device.

v0:
```python
import jax
import jax.numpy as jnp
from jax import lax
from jax.sharding import PartitionSpec as P

HEADS = 48
HD = 128


def contract_last(left, right):
    return lax.dot_general(
        left, right, (((1,), (1,)), ((), ())), preferred_element_type=jnp.float32
    )


def contract_first(left, right):
    return lax.dot_general(
        left, right, (((0,), (0,)), ((), ())), preferred_element_type=jnp.float32
    )


def layer_norm(entries, gain):
    centred = entries - jnp.mean(entries, axis=-1, keepdims=True)
    inverse = lax.rsqrt(jnp.mean(centred * centred, axis=-1, keepdims=True) + 1e-06)
    normal_hat = centred * inverse
    return (normal_hat, inverse, (normal_hat * gain).astype(jnp.bfloat16))


def norm_back(normed_grad, normal_hat, inverse, gain):
    upstream = normed_grad.astype(jnp.float32)
    scaled = upstream * gain
    result = inverse * (
        scaled
        - jnp.mean(scaled, axis=-1, keepdims=True)
        - normal_hat * jnp.mean(scaled * normal_hat, axis=-1, keepdims=True)
    )
    return (result.astype(jnp.bfloat16), jnp.sum(upstream * normal_hat, axis=-2))


def attend(query_normed, key_normed, head_values, upstream):
    factor = query_normed.shape[-1] ** (-0.5)
    scores = contract_last(query_normed, key_normed) * factor
    raised = jnp.exp(scores)
    weights = raised / jnp.sum(raised, axis=-1, keepdims=True)
    weights_low = weights.astype(jnp.bfloat16)
    attended = jnp.dot(weights_low, head_values, preferred_element_type=jnp.float32).astype(
        jnp.bfloat16
    )
    value_grad = contract_first(weights_low, upstream).astype(jnp.bfloat16)
    weights_grad = contract_last(upstream, head_values)
    inner = jnp.sum(weights * weights_grad, axis=-1, keepdims=True)
    score_grad = (weights * (weights_grad - inner)).astype(jnp.bfloat16)
    query_side = (
        jnp.dot(score_grad, key_normed, preferred_element_type=jnp.float32) * factor
    ).astype(jnp.bfloat16)
    key_side = (contract_first(score_grad, query_normed) * factor).astype(jnp.bfloat16)
    return (attended, query_side, key_side, value_grad)


def to_pairs(tokens_layout):
    view_count, token_count, width = tokens_layout.shape
    shaped = tokens_layout.reshape(view_count, token_count, HEADS, HD).transpose(0, 2, 1, 3)
    return shaped.reshape(view_count * HEADS, token_count, HD)


def from_pairs(pairs_layout):
    view_count = pairs_layout.shape[0] // HEADS
    token_count = pairs_layout.shape[1]
    shaped = pairs_layout.reshape(view_count, HEADS, token_count, HD).transpose(0, 2, 1, 3)
    return shaped.reshape(view_count, token_count, HEADS * HD)


def body(queries, keys, values, query_gain, key_gain, cotangent):
    view_count = queries.shape[0]
    gains_query = query_gain.reshape(HEADS, HD)
    gains_key = key_gain.reshape(HEADS, HD)
    tiled_q = jnp.tile(gains_query, (view_count, 1))[:, None, :]
    tiled_k = jnp.tile(gains_key, (view_count, 1))[:, None, :]
    query_hat, query_inv, query_normed = layer_norm(to_pairs(queries).astype(jnp.float32), tiled_q)
    key_hat, key_inv, key_normed = layer_norm(to_pairs(keys).astype(jnp.float32), tiled_k)
    arrived = (
        lax.all_to_all(query_normed, "row", split_axis=0, concat_axis=1, tiled=True),
        lax.all_to_all(key_normed, "row", split_axis=0, concat_axis=1, tiled=True),
        lax.all_to_all(to_pairs(values), "row", split_axis=0, concat_axis=1, tiled=True),
        lax.all_to_all(to_pairs(cotangent), "row", split_axis=0, concat_axis=1, tiled=True),
    )

    def per_pair(members):
        return attend(members[0], members[1], members[2], members[3])

    attended_p, query_side_p, key_side_p, value_grad_p = lax.map(per_pair, arrived)
    attended_t, query_side_t, key_side_t, value_grad_t = (
        lax.all_to_all(attended_p, "row", split_axis=1, concat_axis=0, tiled=True),
        lax.all_to_all(query_side_p, "row", split_axis=1, concat_axis=0, tiled=True),
        lax.all_to_all(key_side_p, "row", split_axis=1, concat_axis=0, tiled=True),
        lax.all_to_all(value_grad_p, "row", split_axis=1, concat_axis=0, tiled=True),
    )
    query_grad, query_terms = norm_back(query_side_t, query_hat, query_inv, tiled_q)
    key_grad, key_terms = norm_back(key_side_t, key_hat, key_inv, tiled_k)
    query_part = query_terms.reshape(view_count, HEADS, HD).sum(axis=0)
    key_part = key_terms.reshape(view_count, HEADS, HD).sum(axis=0)
    query_total, key_total = lax.psum(
        (query_part.reshape(-1), key_part.reshape(-1)), ("row", "col")
    )
    return (
        from_pairs(attended_t),
        from_pairs(query_grad),
        from_pairs(key_grad),
        from_pairs(value_grad_t),
        query_total,
        key_total,
    )


def solution(mesh):
    return jax.shard_map(
        body,
        mesh=mesh,
        in_specs=(
            P("col", "row", None),
            P("col", "row", None),
            P("col", "row", None),
            P(),
            P(),
            P("col", "row", None),
        ),
        out_specs=(
            P("col", "row", None),
            P("col", "row", None),
            P("col", "row", None),
            P("col", "row", None),
            P(),
            P(),
        ),
        check_vma=False,
    )
```

profile of v0, /device:TPU:1, one launch (start us, length us, event | category | flops | bytes accessed | tf_op | source)
XLA Modules:
  0.0 577.3 jit_solution(6844994564976809447)
XLA Ops:
  5.4 9.0 %all-to-all-start = ((bf16[48,128,128]{1,2,0:T(8,128)(2,1)}), bf16[48,128,128]{1,2,0:T(8,128)(2,1)}, u32[]{:S(2)}, u32[]{:S(2)}) async-start(bf16[48,128,128]{1,2,0:T(8,128)(2,1)} %multiply_convert_fusion.2), calls=%async_computation | async-start | bytes 3145728 | tf_op jit(solution)/shard_map/all_to_all | solution.py:82
  19.3 33.6 %all-to-all-done = bf16[48,128,128]{1,2,0:T(8,128)(2,1)} async-done(((bf16[48,128,128]{1,2,0:T(8,128)(2,1)}), bf16[48,128,128]{1,2,0:T(8,128)(2,1)}, u32[]{:S(2)}, u32[]{:S(2)}) %all-to-all-start) | async-done | bytes 1572896 | tf_op jit(solution)/shard_map/all_to_all | solution.py:82
  52.8 4.3 all-to-all-start.1
  59.7 37.8 %all-to-all-done.1 = bf16[48,128,128]{1,2,0:T(8,128)(2,1)} async-done(((bf16[48,128,128]{1,2,0:T(8,128)(2,1)}), bf16[48,128,128]{1,2,0:T(8,128)(2,1)}, u32[]{:S(2)}, u32[]{:S(2)}) %all-to-all-start.1) | async-done | bytes 1572896 | tf_op jit(solution)/shard_map/all_to_all | solution.py:83
  97.5 4.3 all-to-all-start.2
  104.4 35.7 %all-to-all-done.2 = bf16[48,128,128]{1,2,0:T(8,128)(2,1)} async-done(((bf16[48,128,128]{1,2,0:T(8,128)(2,1)}), bf16[48,128,128]{1,2,0:T(8,128)(2,1)}, u32[]{:S(2)}, u32[]{:S(2)}) %all-to-all-start.2) | async-done | bytes 1572896 | tf_op jit(solution)/shard_map/all_to_all | solution.py:84
  140.1 4.5 all-to-all-start.3
  152.5 30.3 %all-to-all-done.3 = bf16[48,128,128]{1,2,0:T(8,128)(2,1)} async-done(((bf16[48,128,128]{1,2,0:T(8,128)(2,1)}), bf16[48,128,128]{1,2,0:T(8,128)(2,1)}, u32[]{:S(2)}, u32[]{:S(2)}) %all-to-all-start.3) | async-done | bytes 1572896 | tf_op jit(solution)/shard_map/all_to_all | solution.py:85
  185.4 88.5 %while.16 = (s32[]{:T(128)}, bf16[6,1024,128]{2,1,0:T(8,128)(2,1)}, bf16[6,1024,128]{2,1,0:T(8,128)(2,1)}, bf16[6,1024,128]{2,1,0:T(8,128)(2,1)}, bf16[6,1024,12...) while((s32[]{:T(128)}, bf16[6,1024,128]{2,1,0:T(8,128)(2,1)}, ...), condition=%wide.region_7.8_spmd, body=%wide.region_4.7_spmd.sunk | while | flops 1629222912 | bytes 38832228 | solution.py:91
  277.7 4.4 all-to-all-start.5
  285.9 44.3 %all-to-all-done.5 = bf16[6,1024,128]{2,0,1:T(8,128)(2,1)} async-done(((bf16[6,1024,128]{2,0,1:T(8,128)(2,1)}), bf16[6,1024,128]{2,0,1:T(8,128)(2,1)}, u32[]{:S(2)}, u32[]{:S(2)}) %all-to-all-start.5) | async-done | bytes 1572896 | tf_op jit(solution)/shard_map/all_to_all | solution.py:94
  330.2 5.0 all-to-all-start.6
  339.0 48.0 %all-to-all-done.6 = bf16[6,1024,128]{2,0,1:T(8,128)(2,1)} async-done(((bf16[6,1024,128]{2,0,1:T(8,128)(2,1)}), bf16[6,1024,128]{2,0,1:T(8,128)(2,1)}, u32[]{:S(2)}, u32[]{:S(2)}) %all-to-all-start.6) | async-done | bytes 1572896 | tf_op jit(solution)/shard_map/all_to_all | solution.py:95
  387.0 4.6 all-to-all-start.4
  403.0 3.9 copy.96
  406.9 33.7 %all-to-all-done.4 = bf16[6,1024,128]{2,0,1:T(8,128)(2,1)} async-done(((bf16[6,1024,128]{2,0,1:T(8,128)(2,1)}), bf16[6,1024,128]{2,0,1:T(8,128)(2,1)}, u32[]{:S(2)}, u32[]{:S(2)}) %all-to-all-start.4) | async-done | bytes 1572896 | tf_op jit(solution)/shard_map/all_to_all | solution.py:93
  440.7 4.3 all-to-all-start.7
  445.0 3.9 convert_bitcast_fusion.1
  448.9 4.4 multiply_reduce_fusion.2
  453.3 3.9 convert_bitcast_fusion
  461.1 3.9 copy.87
  475.0 3.9 copy.76
  491.3 5.3 all-to-all-done.7
  501.1 76.2 %all-reduce = (f32[6144]{0:T(1024)}, f32[6144]{0:T(1024)}) all-reduce(f32[6144]{0:T(1024)S(1)} %reshape.254, f32[6144]{0:T(1024)S(1)} %reshape.255), channel_id=1, replica_groups=mesh['row'=8,'col'=32] {'row','col'}, use_global_device_ids=true, to_apply=%region_13.14 | all-reduce | flops 12288 | bytes 98304 | tf_op jit(solution)/shard_map/psum | solution.py:102
  (120 shorter events, 167.0 us)
Async XLA Ops:
  0.6 2.9 copy-start.3
  5.4 47.4 %all-to-all-start = ((bf16[48,128,128]{1,2,0:T(8,128)(2,1)}), bf16[48,128,128]{1,2,0:T(8,128)(2,1)}, u32[]{:S(2)}, u32[]{:S(2)}) async-start(bf16[48,128,128]{1,2,0:T(8,128)(2,1)} %multiply_convert_fusion.2), calls=%async_computation | async-start | bytes 3145728 | tf_op jit(solution)/shard_map/all_to_all | solution.py:82
  14.4 2.9 copy-start.2
  52.8 44.7 %all-to-all-start.1 = ((bf16[48,128,128]{1,2,0:T(8,128)(2,1)}), bf16[48,128,128]{1,2,0:T(8,128)(2,1)}, u32[]{:S(2)}, u32[]{:S(2)}) async-start(bf16[48,128,128]{1,2,0:T(8,128)(2,1)} %multiply_convert_fusion.1), calls=%async_computation.1 | async-start | bytes 3145728 | tf_op jit(solution)/shard_map/all_to_all | solution.py:83
  97.5 42.5 %all-to-all-start.2 = ((bf16[48,128,128]{1,2,0:T(8,128)(2,1)}), bf16[48,128,128]{1,2,0:T(8,128)(2,1)}, u32[]{:S(2)}, u32[]{:S(2)}) async-start(bf16[48,128,128]{1,2,0:T(8,128)(2,1)} %bitcast.209), calls=%async_computation.2 | async-start | bytes 3145728 | tf_op jit(solution)/shard_map/all_to_all | solution.py:84
  140.1 42.7 %all-to-all-start.3 = ((bf16[48,128,128]{1,2,0:T(8,128)(2,1)}), bf16[48,128,128]{1,2,0:T(8,128)(2,1)}, u32[]{:S(2)}, u32[]{:S(2)}) async-start(bf16[48,128,128]{1,2,0:T(8,128)(2,1)} %bitcast.208), calls=%async_computation.3 | async-start | bytes 3145728 | tf_op jit(solution)/shard_map/all_to_all | solution.py:85
  277.7 52.5 %all-to-all-start.5 = ((bf16[6,1024,128]{2,0,1:T(8,128)(2,1)}), bf16[6,1024,128]{2,0,1:T(8,128)(2,1)}, u32[]{:S(2)}, u32[]{:S(2)}) async-start(bf16[6,1024,128]{2,0,1:T(8,128)(2,1)} %copy.74), calls=%async_computation.5 | async-start | bytes 4194304 | tf_op jit(solution)/shard_map/all_to_all | solution.py:94
  330.2 56.8 %all-to-all-start.6 = ((bf16[6,1024,128]{2,0,1:T(8,128)(2,1)}), bf16[6,1024,128]{2,0,1:T(8,128)(2,1)}, u32[]{:S(2)}, u32[]{:S(2)}) async-start(bf16[6,1024,128]{2,0,1:T(8,128)(2,1)} %copy.85), calls=%async_computation.6 | async-start | bytes 4194304 | tf_op jit(solution)/shard_map/all_to_all | solution.py:95
  387.0 53.7 %all-to-all-start.4 = ((bf16[6,1024,128]{2,0,1:T(8,128)(2,1)}), bf16[6,1024,128]{2,0,1:T(8,128)(2,1)}, u32[]{:S(2)}, u32[]{:S(2)}) async-start(bf16[6,1024,128]{2,0,1:T(8,128)(2,1)} %copy.70), calls=%async_computation.4 | async-start | bytes 4194304 | tf_op jit(solution)/shard_map/all_to_all | solution.py:93
  440.7 55.9 %all-to-all-start.7 = ((bf16[6,1024,128]{2,0,1:T(8,128)(2,1)}), bf16[6,1024,128]{2,0,1:T(8,128)(2,1)}, u32[]{:S(2)}, u32[]{:S(2)}) async-start(bf16[6,1024,128]{2,0,1:T(8,128)(2,1)} %copy.96), calls=%async_computation.7 | async-start | bytes 4194304 | tf_op jit(solution)/shard_map/all_to_all | solution.py:96
  445.0 3.9 copy-start.1
  453.3 3.9 copy-start
  472.3 2.6 copy-start.4
where the time goes:
time: 579 us; the launch traced here: 577 us
  waiting for transfers between devices  269 us (46%)
  matrix products  81.3 us (14%)
  blocking collectives  76.2 us (13%)
  local copies, waits for them, and re-layouts  70.3 us (12%)
  starting transfers between devices  40.3 us (7%)
  other arithmetic  39.3 us (7%)
    psum x1, blocking collectives, body(): lax.psum((query_part.reshape(-1), key_part.reshape(-1)), ('row', 'col'))  76.2 us
    all_to_all x1, waiting for transfers between devices, body(): lax.all_to_all(key_side_p, 'row', split_axis=1, concat_axis=0, tiled=True)  48 us
    all_to_all x1, waiting for transfers between devices, body(): lax.all_to_all(query_side_p, 'row', split_axis=1, concat_axis=0, tiled=True)  44.3 us
    all_to_all x1, waiting for transfers between devices, body(): lax.all_to_all(key_normed, 'row', split_axis=0, concat_axis=1, tiled=True)  37.8 us
    all_to_all x1, waiting for transfers between devices, body(): lax.all_to_all(to_pairs(values), 'row', split_axis=0, concat_axis=1, tile...  35.7 us
    all_to_all x1, waiting for transfers between devices, body(): lax.all_to_all(attended_p, 'row', split_axis=1, concat_axis=0, tiled=True)  33.7 us
    all_to_all x1, waiting for transfers between devices, body(): lax.all_to_all(query_normed, 'row', split_axis=0, concat_axis=1, tiled=True)  33.6 us
    all_to_all x1, waiting for transfers between devices, body(): lax.all_to_all(to_pairs(cotangent), 'row', split_axis=0, concat_axis=1, t...  30.3 us
  transfers between devices with their start and end apart: 8, of which 8 were waited for; matrix products, arithmetic and copies ran while one was open for 15% of the time, Pallas kernels for 0%

commit v1 on v0

v1 whole, which is shorter than its diff:
```python
import functools

import jax
import jax.numpy as jnp
from jax import lax
from jax.experimental import pallas as pl
from jax.experimental.pallas import tpu as pltpu
from jax.sharding import PartitionSpec as P

HEADS = 48
HD = 128
ROWS = 8
MINE = HEADS // ROWS
TOK = 128
LENGTH = ROWS * TOK
WIDE = MINE * HD
BLK = 256
NEAR = 8
FAR = 4
ORDER = (4, 3, 5, 2, 6, 1, 7)
EARLY = 3
FACTOR = HD**-0.5
LOG2E = 1.4426950408889634
MESH = pl.DeviceIdType.MESH


def nn(left, right):
    return lax.dot_general(left, right, (((1,), (0,)), ((), ())), preferred_element_type=jnp.float32)


def nt(left, right):
    return lax.dot_general(left, right, (((1,), (1,)), ((), ())), preferred_element_type=jnp.float32)


def normalise(entries):
    centred = entries - jnp.mean(entries, axis=-1, keepdims=True)
    inverse = lax.rsqrt(jnp.mean(centred * centred, axis=-1, keepdims=True) + 1e-06)
    return centred * inverse, inverse


def norm_back(side, hat, inverse, gain):
    upstream = side.astype(jnp.float32)
    scaled = upstream * gain
    result = inverse * (
        scaled
        - jnp.mean(scaled, axis=-1, keepdims=True)
        - hat * jnp.mean(scaled * hat, axis=-1, keepdims=True)
    )
    return result.astype(jnp.bfloat16), jnp.sum(upstream * hat, axis=0, keepdims=True)


def drain(ref, sem):
    pltpu.make_async_copy(ref, ref, sem).wait()


def kernel(
    q_ref, k_ref, v_ref, g_ref, qgain_ref, kgain_ref,
    att_ref, dq_ref, dk_ref, dv_ref, gq_ref, gk_ref,
    land, res, qhat, khat, qinv, kinv, qn, kn, knt, vt, dk_acc, dv_acc,
    part, land1, sum1, land2, sum2, land3,
    f_send, f_recv, own_in, r_send, r_recv, own_out, g_send, g_recv,
):
    me = lax.axis_index("row")
    col = lax.axis_index("col")
    near = lax.rem(col, NEAR)
    far = lax.div(col, NEAR)
    sources = (q_ref, k_ref, v_ref, g_ref)
    targets = (att_ref, dq_ref, dk_ref, dv_ref)

    def row_peer(d):
        return lax.rem(me + d, ROWS)

    def near_peer(d):
        return far * NEAR + lax.rem(near + d, NEAR)

    def far_peer(d):
        return lax.rem(far + d, FAR) * NEAR + near

    barrier = pltpu.get_barrier_semaphore()
    for d in range(1, ROWS):
        pl.semaphore_signal(barrier, inc=1, device_id=(row_peer(d), col), device_id_type=MESH)
    for d in range(1, NEAR):
        pl.semaphore_signal(barrier, inc=1, device_id=(me, near_peer(d)), device_id_type=MESH)
    for d in range(1, FAR):
        pl.semaphore_signal(barrier, inc=1, device_id=(me, far_peer(d)), device_id_type=MESH)
    pl.semaphore_wait(barrier, ROWS + NEAR + FAR - 3)

    def columns(owner, h):
        return pl.ds(pl.multiple_of(owner * WIDE + h * HD, HD), HD)

    def rows(owner):
        return pl.ds(pl.multiple_of(owner * TOK, TOK), TOK)

    def send_forward(h, carry):
        for d in ORDER:
            peer = row_peer(d)
            for t in range(4):
                pltpu.make_async_remote_copy(
                    src_ref=sources[t].at[0, :, columns(peer, h)],
                    dst_ref=land.at[h, t, rows(me), :],
                    send_sem=f_send,
                    recv_sem=f_recv.at[h],
                    device_id=(peer, col),
                    device_id_type=MESH,
                ).start()
        for t in range(4):
            pltpu.make_async_copy(
                sources[t].at[0, :, columns(me, h)], land.at[h, t, rows(me), :], own_in.at[h]
            ).start()
        return carry

    lax.fori_loop(0, MINE, send_forward, 0)

    def send_back(h):
        for d in ORDER:
            peer = row_peer(d)
            for t in range(4):
                pltpu.make_async_remote_copy(
                    src_ref=res.at[h, t, rows(peer), :],
                    dst_ref=targets[t].at[0, :, columns(me, h)],
                    send_sem=r_send,
                    recv_sem=r_recv.at[t],
                    device_id=(peer, col),
                    device_id_type=MESH,
                ).start()
        for t in range(4):
            pltpu.make_async_copy(
                res.at[h, t, rows(me), :], targets[t].at[0, :, columns(me, h)], own_out
            ).start()

    part[...] = jnp.zeros_like(part)

    def one_head(h, carry):
        drain(land.at[h, :, pl.ds(0, LENGTH - TOK), :], f_recv.at[h])
        drain(land.at[h, :, pl.ds(0, TOK), :], own_in.at[h])
        gain_q = qgain_ref[pl.ds(me * MINE + h, 1), :]
        gain_k = kgain_ref[pl.ds(me * MINE + h, 1), :]
        hat, inverse = normalise(land[h, 0].astype(jnp.float32))
        qhat[...] = hat
        qinv[...] = inverse
        qn[...] = (hat * gain_q).astype(jnp.bfloat16)
        hat, inverse = normalise(land[h, 1].astype(jnp.float32))
        khat[...] = hat
        kinv[...] = inverse
        normed = hat * gain_k
        kn[...] = normed.astype(jnp.bfloat16)
        knt[...] = normed.T.astype(jnp.bfloat16)
        vt[...] = land[h, 2].astype(jnp.float32).T.astype(jnp.bfloat16)
        dk_acc[...] = jnp.zeros_like(dk_acc)
        dv_acc[...] = jnp.zeros_like(dv_acc)

        def block(b, total):
            mine = pl.ds(pl.multiple_of(b * BLK, BLK), BLK)
            q_blk = qn[mine, :]
            g_blk = land[h, 3, mine, :]
            raised = jnp.exp2(nt(kn[...], q_blk) * (FACTOR * LOG2E))
            weights = raised * (1.0 / jnp.sum(raised, axis=0, keepdims=True))
            low = weights.astype(jnp.bfloat16)
            res[h, 0, mine, :] = nn(vt[...], low).T.astype(jnp.bfloat16)
            dv_acc[...] += nn(low, g_blk)
            weights_grad = nt(land[h, 2], g_blk)
            inner = jnp.sum(weights * weights_grad, axis=0, keepdims=True)
            score_grad = (weights * (weights_grad - inner)).astype(jnp.bfloat16)
            dk_acc[...] += nn(score_grad, q_blk)
            side = (nn(knt[...], score_grad) * FACTOR).T.astype(jnp.bfloat16)
            grad, term = norm_back(side, qhat[mine, :], qinv[mine, :], gain_q)
            res[h, 1, mine, :] = grad
            return total + term

        total_q = lax.fori_loop(0, LENGTH // BLK, block, jnp.zeros((1, HD), jnp.float32))
        res[h, 3] = dv_acc[...].astype(jnp.bfloat16)
        side = (dk_acc[...] * FACTOR).astype(jnp.bfloat16)
        grad, total_k = norm_back(side, khat[...], kinv[...], gain_k)
        res[h, 2] = grad
        part[pl.ds(h, 1), :] = total_q
        part[pl.ds(8 + h, 1), :] = total_k

        @pl.when(h < EARLY)
        def _():
            send_back(h)

        return carry

    lax.fori_loop(0, MINE, one_head, 0)

    def share(stage, source, slots, slot, peers):
        for device in peers:
            pltpu.make_async_remote_copy(
                src_ref=source,
                dst_ref=slots.at[slot],
                send_sem=g_send.at[stage],
                recv_sem=g_recv.at[stage],
                device_id=device,
                device_id_type=MESH,
            ).start()
        slots[slot] = source[...]

    def shared(stage, slots, count):
        drain(slots.at[pl.ds(0, count - 1)], g_recv.at[stage])

    share(0, part, land1, near, [(me, near_peer(d)) for d in range(1, NEAR)])
    send_back(3)
    shared(0, land1, NEAR)
    sum1[...] = jnp.sum(land1[...], axis=0)
    share(1, sum1, land2, far, [(me, far_peer(d)) for d in range(1, FAR)])
    send_back(4)
    shared(1, land2, FAR)
    sum2[...] = jnp.sum(land2[...], axis=0)
    share(2, sum2, land3, me, [(row_peer(d), col) for d in range(1, ROWS)])
    send_back(5)
    shared(2, land3, ROWS)
    for r in range(ROWS):
        gq_ref[r * MINE : (r + 1) * MINE, :] = land3[r, 0:MINE, :]
        gk_ref[r * MINE : (r + 1) * MINE, :] = land3[r, 8 : 8 + MINE, :]
    drain(land1.at[pl.ds(0, NEAR - 1)], g_send.at[0])
    drain(land2.at[pl.ds(0, FAR - 1)], g_send.at[1])
    drain(land3.at[pl.ds(0, ROWS - 1)], g_send.at[2])
    drain(land.at[:, :, pl.ds(0, LENGTH - TOK), :], f_send)
    drain(res.at[:, :, pl.ds(0, LENGTH - TOK), :], r_send)
    drain(res.at[:, :, pl.ds(0, TOK), :], own_out)
    for t in range(4):
        drain(targets[t].at[0, :, pl.ds(0, HEADS * HD - WIDE)], r_recv.at[t])


def body(queries, keys, values, query_gain, key_gain, cotangent):
    big = jax.ShapeDtypeStruct(queries.shape, jnp.bfloat16)
    small = jax.ShapeDtypeStruct((HEADS, HD), jnp.float32)
    hbm = pl.BlockSpec(memory_space=pl.ANY)
    vmem = pl.BlockSpec(memory_space=pltpu.VMEM)
    token_f32 = pltpu.VMEM((LENGTH, HD), jnp.float32)
    token_bf16 = pltpu.VMEM((LENGTH, HD), jnp.bfloat16)
    column = pltpu.VMEM((LENGTH, 1), jnp.float32)
    turned = pltpu.VMEM((HD, LENGTH), jnp.bfloat16)
    blocks = pltpu.VMEM((MINE, 4, LENGTH, HD), jnp.bfloat16)
    dma = pltpu.SemaphoreType.DMA
    attended, query_grad, key_grad, value_grad, query_total, key_total = pl.pallas_call(
        kernel,
        out_shape=(big, big, big, big, small, small),
        in_specs=[hbm] * 4 + [vmem] * 2,
        out_specs=(hbm, hbm, hbm, hbm, vmem, vmem),
        scratch_shapes=[
            blocks, blocks, token_f32, token_f32, column, column, token_bf16, token_bf16,
            turned, turned, token_f32, token_f32,
            pltpu.VMEM((16, HD), jnp.float32),
            pltpu.VMEM((NEAR, 16, HD), jnp.float32),
            pltpu.VMEM((16, HD), jnp.float32),
            pltpu.VMEM((FAR, 16, HD), jnp.float32),
            pltpu.VMEM((16, HD), jnp.float32),
            pltpu.VMEM((ROWS, 16, HD), jnp.float32),
            dma, dma((MINE,)), dma((MINE,)), dma, dma((4,)), dma, dma((3,)), dma((3,)),
        ],
        compiler_params=pltpu.CompilerParams(
            collective_id=0, has_side_effects=True, vmem_limit_bytes=56 * 2**20
        ),
        cost_estimate=pl.CostEstimate(
            flops=12 * MINE * LENGTH * LENGTH * HD,
            bytes_accessed=16 * TOK * HEADS * HD,
            transcendentals=MINE * LENGTH * LENGTH,
        ),
        name="attention_exchange",
    )(
        queries, keys, values, cotangent,
        query_gain.reshape(HEADS, HD), key_gain.reshape(HEADS, HD),
    )
    return (
        attended, query_grad, key_grad, value_grad,
        query_total.reshape(-1), key_total.reshape(-1),
    )


def solution(mesh):
    return jax.shard_map(
        body,
        mesh=mesh,
        in_specs=(
            P("col", "row", None),
            P("col", "row", None),
            P("col", "row", None),
            P(),
            P(),
            P("col", "row", None),
        ),
        out_specs=(
            P("col", "row", None),
            P("col", "row", None),
            P("col", "row", None),
            P("col", "row", None),
            P(),
            P(),
        ),
        check_vma=False,
    )
```

time: 579 us -> 293 us (0.51)
  Pallas kernels: 0 us -> 283 us
  waiting for transfers between devices: 269 us -> 0 us
  matrix products: 81.3 us -> 0 us
  blocking collectives: 76.2 us -> 0 us
  local copies, waits for them, and re-layouts: 70.3 us -> 9.13 us
  starting transfers between devices: 40.3 us -> 0 us
  other arithmetic: 39.3 us -> 0 us
    pallas_call x0 -> x1, Pallas kernels: none -> 283 us  [body(): pl.pallas_call(kernel, out_shape=(big, big, big, big, small, small), in_s...]
    all_to_all x8 -> x0, waiting for transfers between devices: 269 us -> none  [the longest x1 48 us: body(): lax.all_to_all(key_side_p, 'row', split_axis=1, concat_axis=0, tiled=True)]
    dot_general x36 -> x0, matrix products: 81.3 us -> none  [the longest x12 29 us: contract_first(): lax.dot_general(left, right, (((0,), (0,)), ((), ())), preferred_element_...]
    psum x1 -> x0, blocking collectives: 76.2 us -> none  [body(): lax.psum((query_part.reshape(-1), key_part.reshape(-1)), ('row', 'col'))]
    all_to_all x8 -> x0, starting transfers between devices: 40.3 us -> none  [the longest x1 9.01 us: body(): lax.all_to_all(query_normed, 'row', split_axis=0, concat_axis=1, tiled=True)]
    convert_element_type x14 -> x0, other arithmetic: 29.2 us -> none  [the longest x2 7.74 us: norm_back(): upstream = normed_grad.astype(jnp.float32)]
    convert_element_type x6 -> x0, local copies, waits for them, and re-layouts: 22.2 us -> none  [the longest x4 15 us: norm_back(): upstream = normed_grad.astype(jnp.float32)]
    while x4 -> x0, local copies, waits for them, and re-layouts: 15.3 us -> none  [body(): lax.map(per_pair, arrived)]
  transfers between devices with their start and end apart: 8 -> 0, of which waited for: 8 -> 0; matrix products, arithmetic and copies ran while one was open for 15% -> 0% of each run, Pallas kernels for 0% -> 0%
where the time goes in v1:
time: 293 us
  Pallas kernels  283 us (97%)
  local copies, waits for them, and re-layouts  9.13 us (3%)
    pallas_call x1, Pallas kernels, body(): pl.pallas_call(kernel, out_shape=(big, big, big, big, small, small), in_s...  283 us
    unnamed x16, local copies, waits for them, and re-layouts  9.13 us

profile of v1, /device:TPU:1, one launch (start us, length us, event | category | flops | bytes accessed | tf_op | source)
XLA Modules:
  0.0 293.3 jit_solution(3627356322186612852)
XLA Ops:
  0.6 283.5 %attention_exchange.1 = (bf16[1,128,6144]{2,1,0:T(8,128)(2,1)}, bf16[1,128,6144]{2,1,0:T(8,128)(2,1)}, bf16[1,128,6144]{2,1,0:T(8,128)(2,1)}, bf16[1,128,6144]{2...) custom-call(bf16[1,128,6144]{2,1,0:T(8,128)(2,1)} %q_ref.1, bf16[1,128,6144]{2,1,0:T(8,128)(2,1)} %k_ref.1, ...), custom_call_target="tpu_custom_call" | custom-call | flops 9663676416 | bytes 12582912 | tf_op jit(solution)/shard_map/attention_exchange/pallas_call | solution.py:236
  284.1 0.0 copy-start.2
  284.1 2.8 copy.18
  286.9 0.0 copy-done.2
  286.9 0.0 copy-start.1
  286.9 1.1 copy.19
  288.1 0.8 copy-done.1
  288.9 0.0 copy-start
  288.9 1.1 copy.20
  290.0 0.8 copy-done
  290.9 0.0 copy-start.4
  290.9 0.0 copy-start.3
  290.9 1.1 copy.21
  292.0 0.0 copy-done.4
  292.0 0.6 copy.22
  292.6 0.0 copy-done.3
  292.6 0.6 copy.23
Async XLA Ops:
  284.1 2.8 copy-start.2
  286.9 2.0 copy-start.1
  288.9 2.0 copy-start
  290.9 1.1 copy-start.4
  290.9 1.8 copy-start.3

commit v2 on v1

--- a/solution.py
+++ b/solution.py
@@ -54,11 +54,11 @@
 
 
 def kernel(
-    q_ref, k_ref, v_ref, g_ref, qgain_ref, kgain_ref,
+    q_ref, k_ref, v_ref, g_ref, qgain_hbm, kgain_hbm,
     att_ref, dq_ref, dk_ref, dv_ref, gq_ref, gk_ref,
     land, res, qhat, khat, qinv, kinv, qn, kn, knt, vt, dk_acc, dv_acc,
-    part, land1, sum1, land2, sum2, land3,
-    f_send, f_recv, own_in, r_send, r_recv, own_out, g_send, g_recv,
+    part, land1, sum1, land2, sum2, land3, total_q, total_k, qgain_ref, kgain_ref,
+    f_send, f_recv, own_in, r_send, r_recv, own_out, g_send, g_recv, g_out, g_in,
 ):
     me = lax.axis_index("row")
     col = lax.axis_index("col")
@@ -75,6 +75,9 @@
 
     def far_peer(d):
         return lax.rem(far + d, FAR) * NEAR + near
+
+    pltpu.make_async_copy(qgain_hbm, qgain_ref, g_in.at[0]).start()
+    pltpu.make_async_copy(kgain_hbm, kgain_ref, g_in.at[1]).start()
 
     barrier = pltpu.get_barrier_semaphore()
     for d in range(1, ROWS):
@@ -129,6 +132,8 @@
             ).start()
 
     part[...] = jnp.zeros_like(part)
+    drain(qgain_ref, g_in.at[0])
+    drain(kgain_ref, g_in.at[1])
 
     def one_head(h, carry):
         drain(land.at[h, :, pl.ds(0, LENGTH - TOK), :], f_recv.at[h])
@@ -167,13 +172,13 @@
             res[h, 1, mine, :] = grad
             return total + term
 
-        total_q = lax.fori_loop(0, LENGTH // BLK, block, jnp.zeros((1, HD), jnp.float32))
+        sum_q = lax.fori_loop(0, LENGTH // BLK, block, jnp.zeros((1, HD), jnp.float32))
         res[h, 3] = dv_acc[...].astype(jnp.bfloat16)
         side = (dk_acc[...] * FACTOR).astype(jnp.bfloat16)
-        grad, total_k = norm_back(side, khat[...], kinv[...], gain_k)
+        grad, sum_k = norm_back(side, khat[...], kinv[...], gain_k)
         res[h, 2] = grad
-        part[pl.ds(h, 1), :] = total_q
-        part[pl.ds(8 + h, 1), :] = total_k
+        part[pl.ds(h, 1), :] = sum_q
+        part[pl.ds(8 + h, 1), :] = sum_k
 
         @pl.when(h < EARLY)
         def _():
@@ -210,8 +215,12 @@
     send_back(5)
     shared(2, land3, ROWS)
     for r in range(ROWS):
-        gq_ref[r * MINE : (r + 1) * MINE, :] = land3[r, 0:MINE, :]
-        gk_ref[r * MINE : (r + 1) * MINE, :] = land3[r, 8 : 8 + MINE, :]
+        total_q[r * MINE : (r + 1) * MINE, :] = land3[r, 0:MINE, :]
+        total_k[r * MINE : (r + 1) * MINE, :] = land3[r, 8 : 8 + MINE, :]
+    pltpu.make_async_copy(total_q, gq_ref, g_out.at[0]).start()
+    pltpu.make_async_copy(total_k, gk_ref, g_out.at[1]).start()
+    drain(total_q, g_out.at[0])
+    drain(total_k, g_out.at[1])
     drain(land1.at[pl.ds(0, NEAR - 1)], g_send.at[0])
     drain(land2.at[pl.ds(0, FAR - 1)], g_send.at[1])
     drain(land3.at[pl.ds(0, ROWS - 1)], g_send.at[2])
@@ -222,22 +231,35 @@
         drain(targets[t].at[0, :, pl.ds(0, HEADS * HD - WIDE)], r_recv.at[t])
 
 
+def settle(*refs):
+    sems = refs[-1]
+    count = len(refs) // 2
+    copies = [
+        pltpu.make_async_copy(refs[i], refs[count + i], sems.at[i]) for i in range(count)
+    ]
+    for copy in copies:
+        copy.start()
+    for copy in copies:
+        copy.wait()
+
+
 def body(queries, keys, values, query_gain, key_gain, cotangent):
     big = jax.ShapeDtypeStruct(queries.shape, jnp.bfloat16)
     small = jax.ShapeDtypeStruct((HEADS, HD), jnp.float32)
     hbm = pl.BlockSpec(memory_space=pl.ANY)
-    vmem = pl.BlockSpec(memory_space=pltpu.VMEM)
     token_f32 = pltpu.VMEM((LENGTH, HD), jnp.float32)
     token_bf16 = pltpu.VMEM((LENGTH, HD), jnp.bfloat16)
     column = pltpu.VMEM((LENGTH, 1), jnp.float32)
     turned = pltpu.VMEM((HD, LENGTH), jnp.bfloat16)
     blocks = pltpu.VMEM((MINE, 4, LENGTH, HD), jnp.bfloat16)
     dma = pltpu.SemaphoreType.DMA
-    attended, query_grad, key_grad, value_grad, query_total, key_total = pl.pallas_call(
+    held = pltpu.VMEM(queries.shape, jnp.bfloat16)
+    held_small = pltpu.VMEM((HEADS, HD), jnp.float32)
+    results = pl.pallas_call(
         kernel,
-        out_shape=(big, big, big, big, small, small),
-        in_specs=[hbm] * 4 + [vmem] * 2,
-        out_specs=(hbm, hbm, hbm, hbm, vmem, vmem),
+        out_shape=(held, held, held, held, held_small, held_small),
+        in_specs=[hbm] * 6,
+        out_specs=(hbm,) * 6,
         scratch_shapes=[
             blocks, blocks, token_f32, token_f32, column, column, token_bf16, token_bf16,
             turned, turned, token_f32, token_f32,
@@ -247,10 +269,14 @@
             pltpu.VMEM((FAR, 16, HD), jnp.float32),
             pltpu.VMEM((16, HD), jnp.float32),
             pltpu.VMEM((ROWS, 16, HD), jnp.float32),
-            dma, dma((MINE,)), dma((MINE,)), dma, dma((4,)), dma, dma((3,)), dma((3,)),
+            pltpu.VMEM((HEADS, HD), jnp.float32),
+            pltpu.VMEM((HEADS, HD), jnp.float32),
+            pltpu.VMEM((HEADS, HD), jnp.float32),
+            pltpu.VMEM((HEADS, HD), jnp.float32),
+            dma, dma((MINE,)), dma((MINE,)), dma, dma((4,)), dma, dma((3,)), dma((3,)), dma((2,)), dma((2,)),
         ],
         compiler_params=pltpu.CompilerParams(
-            collective_id=0, has_side_effects=True, vmem_limit_bytes=56 * 2**20
+            collective_id=0, has_side_effects=True, vmem_limit_bytes=40 * 2**20
         ),
         cost_estimate=pl.CostEstimate(
             flops=12 * MINE * LENGTH * LENGTH * HD,
@@ -259,9 +285,23 @@
         ),
         name="attention_exchange",
     )(
-        queries, keys, values, cotangent,
-        query_gain.reshape(HEADS, HD), key_gain.reshape(HEADS, HD),
+        *(
+            pltpu.with_memory_space_constraint(operand, pltpu.HBM)
+            for operand in (
+                queries, keys, values, cotangent,
+                query_gain.reshape(HEADS, HD), key_gain.reshape(HEADS, HD),
+            )
+        )
     )
+    attended, query_grad, key_grad, value_grad, query_total, key_total = pl.pallas_call(
+        settle,
+        out_shape=(big, big, big, big, small, small),
+        in_specs=[hbm] * 6,
+        out_specs=(hbm,) * 6,
+        scratch_shapes=[dma((6,))],
+        compiler_params=pltpu.CompilerParams(vmem_limit_bytes=2**20),
+        name="settle",
+    )(*(pltpu.with_memory_space_constraint(result, pltpu.VMEM) for result in results))
     return (
         attended, query_grad, key_grad, value_grad,
         query_total.reshape(-1), key_total.reshape(-1),

time: 293 us -> 286 us (0.976)
  local copies, waits for them, and re-layouts: 9.13 us -> 0 us
    unnamed x16 -> x0, local copies, waits for them, and re-layouts: 9.13 us -> none
    pallas_call x1 -> x2, Pallas kernels: 283 us -> 285 us  [the longest x1 282 us: body(): pl.pallas_call(kernel, out_shape=(held, held, held, held, held_small, hel...]
where the time goes in v2:
time: 286 us
  Pallas kernels  285 us (100%)
    pallas_call x1, Pallas kernels, body(): pl.pallas_call(kernel, out_shape=(held, held, held, held, held_small, hel...  282 us

profile of v2, /device:TPU:1, one launch (start us, length us, event | category | flops | bytes accessed | tf_op | source)
XLA Modules:
  0.0 285.5 jit_solution(8472843450547239604)
XLA Ops:
  0.6 282.1 %attention_exchange.1 = (bf16[1,128,6144]{2,1,0:T(8,128)(2,1)S(1)}, bf16[1,128,6144]{2,1,0:T(8,128)(2,1)S(1)}, bf16[1,128,6144]{2,1,0:T(8,128)(2,1)S(1)}, bf16[1...) custom-call(bf16[1,128,6144]{2,1,0:T(8,128)(2,1)} %q_ref.1, ...), custom_call_target="tpu_custom_call" | custom-call | flops 9663676416 | bytes 12582912 | tf_op jit(solution)/shard_map/attention_exchange/pallas_call | solution.py:258
  282.8 2.8 settle.1

commit v3 on v2

--- a/solution.py
+++ b/solution.py
@@ -18,7 +18,7 @@
 NEAR = 8
 FAR = 4
 ORDER = (4, 3, 5, 2, 6, 1, 7)
-EARLY = 3
+EARLY = 2
 FACTOR = HD**-0.5
 LOG2E = 1.4426950408889634
 MESH = pl.DeviceIdType.MESH
@@ -57,8 +57,8 @@
     q_ref, k_ref, v_ref, g_ref, qgain_hbm, kgain_hbm,
     att_ref, dq_ref, dk_ref, dv_ref, gq_ref, gk_ref,
     land, res, qhat, khat, qinv, kinv, qn, kn, knt, vt, dk_acc, dv_acc,
-    part, land1, sum1, land2, sum2, land3, total_q, total_k, qgain_ref, kgain_ref,
-    f_send, f_recv, own_in, r_send, r_recv, own_out, g_send, g_recv, g_out, g_in,
+    part, land1, sum1, land2, sum2, land3, land4, total_q, total_k, qgain_ref, kgain_ref,
+    f_send, f_recv, own_in, r_send, r_recv, own_out, g_send, g_recv, g_out, g_in, rings_here,
 ):
     me = lax.axis_index("row")
     col = lax.axis_index("col")
@@ -82,11 +82,20 @@
     barrier = pltpu.get_barrier_semaphore()
     for d in range(1, ROWS):
         pl.semaphore_signal(barrier, inc=1, device_id=(row_peer(d), col), device_id_type=MESH)
-    for d in range(1, NEAR):
-        pl.semaphore_signal(barrier, inc=1, device_id=(me, near_peer(d)), device_id_type=MESH)
-    for d in range(1, FAR):
-        pl.semaphore_signal(barrier, inc=1, device_id=(me, far_peer(d)), device_id_type=MESH)
-    pl.semaphore_wait(barrier, ROWS + NEAR + FAR - 3)
+    plane_peers = [(me, near_peer(d)) for d in range(1, NEAR)]
+    plane_peers += [(me, far_peer(d)) for d in range(1, FAR)]
+
+    @pl.when(me == 0)
+    def _():
+        for device in plane_peers:
+            pl.semaphore_signal(barrier, inc=1, device_id=device, device_id_type=MESH)
+        pl.semaphore_wait(barrier, ROWS - 1 + len(plane_peers))
+        for device in plane_peers:
+            pl.semaphore_signal(rings_here, inc=1, device_id=device, device_id_type=MESH)
+
+    @pl.when(me != 0)
+    def _():
+        pl.semaphore_wait(barrier, ROWS - 1)
 
     def columns(owner, h):
         return pl.ds(pl.multiple_of(owner * WIDE + h * HD, HD), HD)
@@ -177,8 +186,8 @@
         side = (dk_acc[...] * FACTOR).astype(jnp.bfloat16)
         grad, sum_k = norm_back(side, khat[...], kinv[...], gain_k)
         res[h, 2] = grad
-        part[pl.ds(h, 1), :] = sum_q
-        part[pl.ds(8 + h, 1), :] = sum_k
+        part[lax.div(h, 2), pl.ds(lax.rem(h, 2), 1), :] = sum_q
+        part[MINE // 2 + lax.div(h, 2), pl.ds(lax.rem(h, 2), 1), :] = sum_k
 
         @pl.when(h < EARLY)
         def _():
@@ -188,35 +197,55 @@
 
     lax.fori_loop(0, MINE, one_head, 0)
 
-    def share(stage, source, slots, slot, peers):
-        for device in peers:
-            pltpu.make_async_remote_copy(
-                src_ref=source,
-                dst_ref=slots.at[slot],
-                send_sem=g_send.at[stage],
-                recv_sem=g_recv.at[stage],
-                device_id=device,
-                device_id_type=MESH,
-            ).start()
-        slots[slot] = source[...]
+    @pl.when(me == 0)
+    def _():
+        pl.semaphore_wait(rings_here, len(plane_peers))
+        for d in range(1, ROWS):
+            pl.semaphore_signal(rings_here, inc=1, device_id=(row_peer(d), col), device_id_type=MESH)
+
+    @pl.when(me != 0)
+    def _():
+        pl.semaphore_wait(rings_here, 1)
+
+    def share(stage, source, slots, slot, device):
+        pltpu.make_async_remote_copy(
+            src_ref=source,
+            dst_ref=slots.at[slot],
+            send_sem=g_send.at[stage],
+            recv_sem=g_recv.at[stage],
+            device_id=device,
+            device_id_type=MESH,
+        ).start()
 
     def shared(stage, slots, count):
         drain(slots.at[pl.ds(0, count - 1)], g_recv.at[stage])
 
-    share(0, part, land1, near, [(me, near_peer(d)) for d in range(1, NEAR)])
-    send_back(3)
+    for d in range(1, NEAR):
+        share(0, part.at[lax.rem(near + d, NEAR)], land1, near, (me, near_peer(d)))
+    land1[near] = part[near]
+    send_back(2)
     shared(0, land1, NEAR)
     sum1[...] = jnp.sum(land1[...], axis=0)
-    share(1, sum1, land2, far, [(me, far_peer(d)) for d in range(1, FAR)])
-    send_back(4)
+    for d in range(1, FAR):
+        share(1, sum1, land2, far, (me, far_peer(d)))
+    land2[far] = sum1[...]
+    send_back(3)
     shared(1, land2, FAR)
     sum2[...] = jnp.sum(land2[...], axis=0)
-    share(2, sum2, land3, me, [(row_peer(d), col) for d in range(1, ROWS)])
+    for d in range(1, ROWS):
+        share(2, sum2, land3, me, (row_peer(d), col))
+    land3[me] = sum2[...]
+    send_back(4)
+    shared(2, land3, ROWS)
+    for d in range(1, NEAR):
+        share(3, land3, land4, near, (me, near_peer(d)))
+    land4[near] = land3[...]
     send_back(5)
-    shared(2, land3, ROWS)
+    shared(3, land4, NEAR)
     for r in range(ROWS):
-        total_q[r * MINE : (r + 1) * MINE, :] = land3[r, 0:MINE, :]
-        total_k[r * MINE : (r + 1) * MINE, :] = land3[r, 8 : 8 + MINE, :]
+        for h in range(0, MINE, 2):
+            total_q[r * MINE + h : r * MINE + h + 2, :] = land4[h // 2, r]
+            total_k[r * MINE + h : r * MINE + h + 2, :] = land4[(MINE + h) // 2, r]
     pltpu.make_async_copy(total_q, gq_ref, g_out.at[0]).start()
     pltpu.make_async_copy(total_k, gk_ref, g_out.at[1]).start()
     drain(total_q, g_out.at[0])
@@ -224,6 +253,7 @@
     drain(land1.at[pl.ds(0, NEAR - 1)], g_send.at[0])
     drain(land2.at[pl.ds(0, FAR - 1)], g_send.at[1])
     drain(land3.at[pl.ds(0, ROWS - 1)], g_send.at[2])
+    drain(land4.at[pl.ds(0, NEAR - 1)], g_send.at[3])
     drain(land.at[:, :, pl.ds(0, LENGTH - TOK), :], f_send)
     drain(res.at[:, :, pl.ds(0, LENGTH - TOK), :], r_send)
     drain(res.at[:, :, pl.ds(0, TOK), :], own_out)
@@ -263,17 +293,19 @@
         scratch_shapes=[
             blocks, blocks, token_f32, token_f32, column, column, token_bf16, token_bf16,
             turned, turned, token_f32, token_f32,
-            pltpu.VMEM((16, HD), jnp.float32),
-            pltpu.VMEM((NEAR, 16, HD), jnp.float32),
-            pltpu.VMEM((16, HD), jnp.float32),
-            pltpu.VMEM((FAR, 16, HD), jnp.float32),
-            pltpu.VMEM((16, HD), jnp.float32),
-            pltpu.VMEM((ROWS, 16, HD), jnp.float32),
+            pltpu.VMEM((NEAR, 2, HD), jnp.float32),
+            pltpu.VMEM((NEAR, 2, HD), jnp.float32),
+            pltpu.VMEM((2, HD), jnp.float32),
+            pltpu.VMEM((FAR, 2, HD), jnp.float32),
+            pltpu.VMEM((2, HD), jnp.float32),
+            pltpu.VMEM((ROWS, 2, HD), jnp.float32),
+            pltpu.VMEM((NEAR, ROWS, 2, HD), jnp.float32),
             pltpu.VMEM((HEADS, HD), jnp.float32),
             pltpu.VMEM((HEADS, HD), jnp.float32),
             pltpu.VMEM((HEADS, HD), jnp.float32),
             pltpu.VMEM((HEADS, HD), jnp.float32),
-            dma, dma((MINE,)), dma((MINE,)), dma, dma((4,)), dma, dma((3,)), dma((3,)), dma((2,)), dma((2,)),
+            dma, dma((MINE,)), dma((MINE,)), dma, dma((4,)), dma, dma((4,)), dma((4,)), dma((2,)), dma((2,)),
+            pltpu.SemaphoreType.REGULAR,
         ],
         compiler_params=pltpu.CompilerParams(
             collective_id=0, has_side_effects=True, vmem_limit_bytes=40 * 2**20

time: 286 us -> 283 us (0.990)
  Pallas kernels: 285 us -> 282 us
where the time goes in v3:
time: 283 us
  Pallas kernels  282 us (100%)
    pallas_call x1, Pallas kernels, body(): pl.pallas_call(kernel, out_shape=(held, held, held, held, held_small, hel...  280 us

profile of v3, /device:TPU:1, one launch (start us, length us, event | category | flops | bytes accessed | tf_op | source)
XLA Modules:
  0.0 283.0 jit_solution(5752849425929862098)
XLA Ops:
  0.6 279.6 %attention_exchange.1 = (bf16[1,128,6144]{2,1,0:T(8,128)(2,1)S(1)}, bf16[1,128,6144]{2,1,0:T(8,128)(2,1)S(1)}, bf16[1,128,6144]{2,1,0:T(8,128)(2,1)S(1)}, bf16[1...) custom-call(bf16[1,128,6144]{2,1,0:T(8,128)(2,1)} %q_ref.1, ...), custom_call_target="tpu_custom_call" | custom-call | flops 9663676416 | bytes 12582912 | tf_op jit(solution)/shard_map/attention_exchange/pallas_call | solution.py:288
  280.2 2.8 settle.1

commit v4 on v3

--- a/solution.py
+++ b/solution.py
@@ -58,7 +58,7 @@
     att_ref, dq_ref, dk_ref, dv_ref, gq_ref, gk_ref,
     land, res, qhat, khat, qinv, kinv, qn, kn, knt, vt, dk_acc, dv_acc,
     part, land1, sum1, land2, sum2, land3, land4, total_q, total_k, qgain_ref, kgain_ref,
-    f_send, f_recv, own_in, r_send, r_recv, own_out, g_send, g_recv, g_out, g_in, rings_here,
+    f_send, f_recv, own_in, r_send, r_recv, own_out, g_send, g_recv, g_out, g_in, rings_here, from_left, from_right,
 ):
     me = lax.axis_index("row")
     col = lax.axis_index("col")
@@ -76,26 +76,23 @@
     def far_peer(d):
         return lax.rem(far + d, FAR) * NEAR + near
 
-    pltpu.make_async_copy(qgain_hbm, qgain_ref, g_in.at[0]).start()
-    pltpu.make_async_copy(kgain_hbm, kgain_ref, g_in.at[1]).start()
-
-    barrier = pltpu.get_barrier_semaphore()
-    for d in range(1, ROWS):
-        pl.semaphore_signal(barrier, inc=1, device_id=(row_peer(d), col), device_id_type=MESH)
+    left, right = (row_peer(ROWS - 1), col), (row_peer(1), col)
     plane_peers = [(me, near_peer(d)) for d in range(1, NEAR)]
     plane_peers += [(me, far_peer(d)) for d in range(1, FAR)]
 
+    barrier = pltpu.get_barrier_semaphore()
+    for device in (left, right):
+        pl.semaphore_signal(barrier, inc=1, device_id=device, device_id_type=MESH)
+
     @pl.when(me == 0)
     def _():
         for device in plane_peers:
             pl.semaphore_signal(barrier, inc=1, device_id=device, device_id_type=MESH)
-        pl.semaphore_wait(barrier, ROWS - 1 + len(plane_peers))
-        for device in plane_peers:
-            pl.semaphore_signal(rings_here, inc=1, device_id=device, device_id_type=MESH)
+        pl.semaphore_wait(barrier, 2 + len(plane_peers))
 
     @pl.when(me != 0)
     def _():
-        pl.semaphore_wait(barrier, ROWS - 1)
+        pl.semaphore_wait(barrier, 2)
 
     def columns(owner, h):
         return pl.ds(pl.multiple_of(owner * WIDE + h * HD, HD), HD)
@@ -103,25 +100,49 @@
     def rows(owner):
         return pl.ds(pl.multiple_of(owner * TOK, TOK), TOK)
 
+    def send_to(h, d):
+        peer = row_peer(d)
+        for t in range(4):
+            pltpu.make_async_remote_copy(
+                src_ref=sources[t].at[0, :, columns(peer, h)],
+                dst_ref=land.at[h, t, rows(me), :],
+                send_sem=f_send,
+                recv_sem=f_recv.at[h],
+                device_id=(peer, col),
+                device_id_type=MESH,
+            ).start()
+
+    for step in range(1, ROWS // 2):
+        pl.semaphore_signal(from_left.at[step - 1], inc=1, device_id=right, device_id_type=MESH)
+        if step < ROWS // 2 - 1:
+            pl.semaphore_signal(from_right.at[step - 1], inc=1, device_id=left, device_id_type=MESH)
+        send_to(0, step)
+        send_to(0, ROWS - step)
+        pl.semaphore_wait(from_left.at[step - 1], 1)
+        if step < ROWS // 2 - 1:
+            pl.semaphore_wait(from_right.at[step - 1], 1)
+    send_to(0, ROWS // 2)
+
     def send_forward(h, carry):
         for d in ORDER:
-            peer = row_peer(d)
-            for t in range(4):
-                pltpu.make_async_remote_copy(
-                    src_ref=sources[t].at[0, :, columns(peer, h)],
-                    dst_ref=land.at[h, t, rows(me), :],
-                    send_sem=f_send,
-                    recv_sem=f_recv.at[h],
-                    device_id=(peer, col),
-                    device_id_type=MESH,
-                ).start()
+            send_to(h, d)
+        return carry
+
+    lax.fori_loop(1, MINE, send_forward, 0)
+
+    def fetch_own(h, carry):
         for t in range(4):
             pltpu.make_async_copy(
                 sources[t].at[0, :, columns(me, h)], land.at[h, t, rows(me), :], own_in.at[h]
             ).start()
         return carry
 
-    lax.fori_loop(0, MINE, send_forward, 0)
+    lax.fori_loop(0, MINE, fetch_own, 0)
+
+    @pl.when(me == 0)
+    def _():
+        for device in plane_peers:
+            pl.semaphore_signal(rings_here, inc=1, device_id=device, device_id_type=MESH)
 
     def send_back(h):
         for d in ORDER:
@@ -140,6 +161,8 @@
                 res.at[h, t, rows(me), :], targets[t].at[0, :, columns(me, h)], own_out
             ).start()
 
+    pltpu.make_async_copy(qgain_hbm, qgain_ref, g_in.at[0]).start()
+    pltpu.make_async_copy(kgain_hbm, kgain_ref, g_in.at[1]).start()
     part[...] = jnp.zeros_like(part)
     drain(qgain_ref, g_in.at[0])
     drain(kgain_ref, g_in.at[1])
@@ -306,6 +329,8 @@
             pltpu.VMEM((HEADS, HD), jnp.float32),
             dma, dma((MINE,)), dma((MINE,)), dma, dma((4,)), dma, dma((4,)), dma((4,)), dma((2,)), dma((2,)),
             pltpu.SemaphoreType.REGULAR,
+            pltpu.SemaphoreType.REGULAR((ROWS // 2 - 1,)),
+            pltpu.SemaphoreType.REGULAR((ROWS // 2 - 2,)),
         ],
         compiler_params=pltpu.CompilerParams(
             collective_id=0, has_side_effects=True, vmem_limit_bytes=40 * 2**20

time: 283 us -> 281 us (level)
  no operation moved by 1% of the time
where the time goes in v4:
time: 281 us
  Pallas kernels  281 us (100%)
    pallas_call x1, Pallas kernels, body(): pl.pallas_call(kernel, out_shape=(held, held, held, held, held_small, hel...  278 us

profile of v4, /device:TPU:1, one launch (start us, length us, event | category | flops | bytes accessed | tf_op | source)
XLA Modules:
  0.0 281.3 jit_solution(12786395875920781103)
XLA Ops:
  0.6 277.9 %attention_exchange.1 = (bf16[1,128,6144]{2,1,0:T(8,128)(2,1)S(1)}, bf16[1,128,6144]{2,1,0:T(8,128)(2,1)S(1)}, bf16[1,128,6144]{2,1,0:T(8,128)(2,1)S(1)}, bf16[1...) custom-call(bf16[1,128,6144]{2,1,0:T(8,128)(2,1)} %q_ref.1, ...), custom_call_target="tpu_custom_call" | custom-call | flops 9663676416 | bytes 12582912 | tf_op jit(solution)/shard_map/attention_exchange/pallas_call | solution.py:311
  278.6 2.8 settle.1

commit v5 on v4

--- a/solution.py
+++ b/solution.py
@@ -55,7 +55,7 @@
 
 def kernel(
     q_ref, k_ref, v_ref, g_ref, qgain_hbm, kgain_hbm,
-    att_ref, dq_ref, dk_ref, dv_ref, gq_ref, gk_ref,
+    back_ref, gq_ref, gk_ref,
     land, res, qhat, khat, qinv, kinv, qn, kn, knt, vt, dk_acc, dv_acc,
     part, land1, sum1, land2, sum2, land3, land4, total_q, total_k, qgain_ref, kgain_ref,
     f_send, f_recv, own_in, r_send, r_recv, own_out, g_send, g_recv, g_out, g_in, rings_here, from_left, from_right,
@@ -65,7 +65,6 @@
     near = lax.rem(col, NEAR)
     far = lax.div(col, NEAR)
     sources = (q_ref, k_ref, v_ref, g_ref)
-    targets = (att_ref, dq_ref, dk_ref, dv_ref)
 
     def row_peer(d):
         return lax.rem(me + d, ROWS)
@@ -147,19 +146,17 @@
     def send_back(h):
         for d in ORDER:
             peer = row_peer(d)
-            for t in range(4):
-                pltpu.make_async_remote_copy(
-                    src_ref=res.at[h, t, rows(peer), :],
-                    dst_ref=targets[t].at[0, :, columns(me, h)],
-                    send_sem=r_send,
-                    recv_sem=r_recv.at[t],
-                    device_id=(peer, col),
-                    device_id_type=MESH,
-                ).start()
-        for t in range(4):
-            pltpu.make_async_copy(
-                res.at[h, t, rows(me), :], targets[t].at[0, :, columns(me, h)], own_out
+            pltpu.make_async_remote_copy(
+                src_ref=res.at[h, :, rows(peer), :],
+                dst_ref=back_ref.at[:, :, columns(me, h)],
+                send_sem=r_send,
+                recv_sem=r_recv,
+                device_id=(peer, col),
+                device_id_type=MESH,
             ).start()
+        pltpu.make_async_copy(
+            res.at[h, :, rows(me), :], back_ref.at[:, :, columns(me, h)], own_out
+        ).start()
 
     pltpu.make_async_copy(qgain_hbm, qgain_ref, g_in.at[0]).start()
     pltpu.make_async_copy(kgain_hbm, kgain_ref, g_in.at[1]).start()
@@ -280,16 +277,13 @@
     drain(land.at[:, :, pl.ds(0, LENGTH - TOK), :], f_send)
     drain(res.at[:, :, pl.ds(0, LENGTH - TOK), :], r_send)
     drain(res.at[:, :, pl.ds(0, TOK), :], own_out)
-    for t in range(4):
-        drain(targets[t].at[0, :, pl.ds(0, HEADS * HD - WIDE)], r_recv.at[t])
-
-
-def settle(*refs):
-    sems = refs[-1]
-    count = len(refs) // 2
-    copies = [
-        pltpu.make_async_copy(refs[i], refs[count + i], sems.at[i]) for i in range(count)
-    ]
+    drain(back_ref.at[:, :, pl.ds(0, HEADS * HD - WIDE)], r_recv)
+
+
+def settle(back_ref, gq_ref, gk_ref, *rest):
+    outs, sems = rest[:-1], rest[-1]
+    held = [back_ref.at[pl.ds(t, 1)] for t in range(4)] + [gq_ref, gk_ref]
+    copies = [pltpu.make_async_copy(held[i], outs[i], sems.at[i]) for i in range(6)]
     for copy in copies:
         copy.start()
     for copy in copies:
@@ -306,13 +300,13 @@
     turned = pltpu.VMEM((HD, LENGTH), jnp.bfloat16)
     blocks = pltpu.VMEM((MINE, 4, LENGTH, HD), jnp.bfloat16)
     dma = pltpu.SemaphoreType.DMA
-    held = pltpu.VMEM(queries.shape, jnp.bfloat16)
+    held = pltpu.VMEM((4, TOK, HEADS * HD), jnp.bfloat16)
     held_small = pltpu.VMEM((HEADS, HD), jnp.float32)
     results = pl.pallas_call(
         kernel,
-        out_shape=(held, held, held, held, held_small, held_small),
+        out_shape=(held, held_small, held_small),
         in_specs=[hbm] * 6,
-        out_specs=(hbm,) * 6,
+        out_specs=(hbm,) * 3,
         scratch_shapes=[
             blocks, blocks, token_f32, token_f32, column, column, token_bf16, token_bf16,
             turned, turned, token_f32, token_f32,
@@ -327,7 +321,7 @@
             pltpu.VMEM((HEADS, HD), jnp.float32),
             pltpu.VMEM((HEADS, HD), jnp.float32),
             pltpu.VMEM((HEADS, HD), jnp.float32),
-            dma, dma((MINE,)), dma((MINE,)), dma, dma((4,)), dma, dma((4,)), dma((4,)), dma((2,)), dma((2,)),
+            dma, dma((MINE,)), dma((MINE,)), dma, dma, dma, dma((4,)), dma((4,)), dma((2,)), dma((2,)),
             pltpu.SemaphoreType.REGULAR,
             pltpu.SemaphoreType.REGULAR((ROWS // 2 - 1,)),
             pltpu.SemaphoreType.REGULAR((ROWS // 2 - 2,)),
@@ -353,7 +347,7 @@
     attended, query_grad, key_grad, value_grad, query_total, key_total = pl.pallas_call(
         settle,
         out_shape=(big, big, big, big, small, small),
-        in_specs=[hbm] * 6,
+        in_specs=[hbm] * 3,
         out_specs=(hbm,) * 6,
         scratch_shapes=[dma((6,))],
         compiler_params=pltpu.CompilerParams(vmem_limit_bytes=2**20),

time: 281 us -> 281 us (level)
  no operation moved by 1% of the time
where the time goes in v5:
time: 281 us
  Pallas kernels  281 us (100%)
    pallas_call x1, Pallas kernels, body(): pl.pallas_call(kernel, out_shape=(held, held_small, held_small), in_specs...  278 us

profile of v5, /device:TPU:1, one launch (start us, length us, event | category | flops | bytes accessed | tf_op | source)
XLA Modules:
  0.0 281.3 jit_solution(6595202678738901571)
XLA Ops:
  0.6 277.9 %attention_exchange.1 = (bf16[4,128,6144]{2,1,0:T(8,128)(2,1)S(1)}, f32[48,128]{1,0:T(8,128)S(1)}, f32[48,128]{1,0:T(8,128)S(1)}) custom-call(bf16[1,128,6144]{2,1,0:T(8,128)(2,1)} %q_ref.1, bf16[1,128,6144]{2,1,0:T(8,128)(2,1)} %k_ref.1, bf16[1,128,6144]{2,1,0:T(8,128)(2,1)} %v_ref.1, bf16[1,128,6144]{2,1,0:T(8,128)(2,1)} %g_ref.1, f32[48,128]{1,0:T(8,128)} %bitcast.4, ...), custom_call_target="tpu_custom_call" | custom-call | flops 9663676416 | bytes 12582912 | tf_op jit(solution)/shard_map/attention_exchange/pallas_call | solution.py:305
  278.5 2.8 settle.1
